TPU v7x, 256 devices: a whole 4x4x8 slice. The times are simulated.
256 devices in a mesh: row: 16 (over z, core), col: 16 (over y, x).
Axes of the slice: x: 4, y: 4, z: 8, core: 2. Of those that a mesh axis runs over, the one named last changes fastest.
Arguments:
- vectors: float32 [2048, 48, 512], P(('row', 'col')), may hold values from -6 to 6
- factor_one: float32 [2048, 47, 2048], P('row', None, 'col'), may hold values from -0.125 to 0.125
- factor_two: float32 [2048, 46, 2048], P('row', None, 'col'), may hold values from -0.125 to 0.125
- block_inverse: float32 [2, 2048, 2048], P(None, 'row', 'col'), may hold values from -1 to 2, as said below
- lumped_mass: float32 [2048, 48], P(('row', 'col')), may hold values from 0.25 to 9.5
Outputs:
- solved: float32 [2048, 48, 512], P(('row', 'col'))
- rotated: float32 [2048, 48, 512], P(('row', 'col'))
Inputs may be any that keep to these rules, and one draw needn't show every extreme that they name: Each block of block_inverse is lower triangular with diagonal entries between 0.5 and 2.
All inputs are finite; a program needn't handle non-finite values.
Results may differ from a plain program's by a relative error of at most 0.00013.
Values sent between devices are 32-bit elements; how exact they have to be, the bound alone decides.
No kernel may reach another device: no remote copies, remote signals or barrier semaphores. Data moves between devices by JAX's collectives and lax.ppermute only.
A program may use at most 128 MiB of HBM per device.

v0:
```python
import jax
import jax.numpy as jnp
from jax import lax
from jax.sharding import PartitionSpec as P

ORDER = 98304


def spread(block, axis, holder):
    block = jnp.where(lax.axis_index(axis) == holder, block, jnp.zeros_like(block))
    return lax.psum(block, axis)


def spread_rows(panel_rows):
    grid_block = lax.all_gather(panel_rows, "col", axis=0, tiled=True)
    per_column = lax.axis_size("row") // lax.axis_size("col")
    column = lax.axis_index("col")
    gathered = spread(grid_block, "row", column * per_column + 0)
    return gathered


def solve_panel(panel_rows, inverse_tile):
    needed = spread_rows(panel_rows)
    partial_value = jnp.dot(
        inverse_tile, needed, precision=lax.Precision.HIGHEST, preferred_element_type=jnp.float32
    )
    return lax.psum_scatter(partial_value, "col", scatter_dimension=0, tiled=True)


def trailing(lower_tile, solved_cols):
    return lax.psum_scatter(
        jnp.einsum(
            "jtq,qk->jtk",
            lower_tile,
            solved_cols,
            precision=lax.Precision.HIGHEST,
            preferred_element_type=jnp.float32,
        ),
        "col",
        scatter_dimension=0,
        tiled=True,
    )


def body(vectors, factor_one, factor_two, block_inverse, lumped_mass):
    highest = lax.Precision.HIGHEST
    panel_one = solve_panel(vectors[:, 0, :], block_inverse[0])
    one_cols = spread_rows(panel_one)
    remain = vectors[:, 1:, :] - trailing(factor_one, one_cols)
    panel_two = solve_panel(remain[:, 0, :], block_inverse[1])
    two_cols = spread_rows(panel_two)
    remaining = remain[:, 1:, :] - trailing(factor_two, two_cols)
    solved = jnp.concatenate([panel_one[:, None, :], panel_two[:, None, :], remaining], axis=1)
    weighted = solved * lumped_mass[:, :, None]
    local_gram = jnp.einsum(
        "jtk,jtl->kl", weighted, solved, precision=highest, preferred_element_type=jnp.float32
    )
    mass_gram = lax.psum(local_gram, ("row", "col")) / ORDER
    factor = jnp.linalg.cholesky(mass_gram)
    flattened = solved.reshape(-1, solved.shape[2])
    rotated = jax.scipy.linalg.solve_triangular(factor, flattened.T, lower=True).T
    return (solved, rotated.reshape(solved.shape))


def solution(mesh):
    placed = (
        P(("row", "col"), None, None),
        P("row", None, "col"),
        P("row", None, "col"),
        P(None, "row", "col"),
        P(("row", "col"), None),
    )
    return jax.shard_map(
        body,
        mesh=mesh,
        in_specs=placed,
        out_specs=(P(("row", "col"), None, None), P(("row", "col"), None, None)),
        check_vma=False,
    )
```

profile of v0, /device:TPU:2, one launch (start us, length us, event | category | flops | bytes accessed | tf_op | source)
XLA Modules:
  0.0 1415.3 jit_solution(13320057616582228687)
XLA Ops:
  8.3 23.8 %all-gather = f32[128,1,512]{2,1,0:T(1,128)S(1)} all-gather(f32[8,1,512]{2,1,0:T(1,128)S(1)} %slice.132), channel_id=2, replica_groups=mesh['row'=16,'col'=16] {'col'}, dimensions={0}, use_global_device_ids=true | all-gather | bytes 278528 | tf_op jit(solution)/shard_map/all_gather | solution.py:15
  33.1 109.6 %all-reduce.11.cloned.1.call-done = f32[128,512]{1,0:T(8,128)} async-done(((f32[128,512]{1,0:T(8,128)}), f32[128,512]{1,0:T(8,128)}) %all-reduce.11.cloned.1.call-update) | async-done | bytes 262160 | tf_op jit(solution)/shard_map/psum | solution.py:11
  142.6 2.2 convolution_bitcast_fusion.4
  145.0 1.3 dynamic-slice.3
  146.9 94.3 %all-reduce.21.cloned.1.call-done = f32[128,512]{0,1:T(8,128)} async-done(((f32[128,512]{0,1:T(8,128)}), f32[128,512]{0,1:T(8,128)}) %all-reduce.21.cloned.1.call-update) | async-done | bytes 262160
  242.3 24.2 %all_gather.13 = f32[128,512]{1,0:T(8,128)} all-gather(f32[8,512]{1,0:T(8,128)S(1)} %copy.41), channel_id=1, replica_groups=mesh['row'=16,'col'=16] {'col'}, dimensions={0}, use_global_device_ids=true | all-gather | bytes 278528 | tf_op jit(solution)/shard_map/all_gather | solution.py:15
  266.5 1.1 copy.42
  268.4 108.2 %all-reduce.13.cloned.1.call-done = f32[128,512]{0,1:T(8,128)} async-done(((f32[128,512]{0,1:T(8,128)}), f32[128,512]{0,1:T(8,128)}) %all-reduce.13.cloned.1.call-update) | async-done | bytes 262160 | tf_op jit(solution)/shard_map/psum | solution.py:11
  376.6 13.6 convolution_bitcast_fusion
  390.2 12.7 copy.43
  403.0 99.3 %reduce-scatter.5.cloned.1.call-done = f32[8,47,512]{2,1,0:T(8,128)} async-done(((f32[128,47,512]{2,1,0:T(8,128)}), f32[8,47,512]{2,1,0:T(8,128)}) %reduce-scatter.5.cloned.1.call-update) | async-done | bytes 770064 | tf_op jit(solution)/shard_map/reduce_scatter | solution.py:31
  502.3 1.5 slice_subtract_fusion.1
  504.7 22.2 %all-gather.1 = f32[128,1,512]{2,1,0:T(1,128)S(1)} all-gather(f32[8,1,512]{2,1,0:T(1,128)S(1)} %slice.149), channel_id=3, replica_groups=mesh['row'=16,'col'=16] {'col'}, dimensions={0}, use_global_device_ids=true | all-gather | bytes 278528 | tf_op jit(solution)/shard_map/all_gather | solution.py:15
  527.9 108.6 %all-reduce.15.cloned.1.call-done = f32[128,512]{1,0:T(8,128)} async-done(((f32[128,512]{1,0:T(8,128)}), f32[128,512]{1,0:T(8,128)}) %all-reduce.15.cloned.1.call-update) | async-done | bytes 262160 | tf_op jit(solution)/shard_map/psum | solution.py:11
  636.6 2.2 convolution_bitcast_fusion.3
  638.9 95.7 %all-reduce.23.cloned.1.call-done = f32[128,512]{0,1:T(8,128)} async-done(((f32[128,512]{0,1:T(8,128)}), f32[128,512]{0,1:T(8,128)}) %all-reduce.23.cloned.1.call-update) | async-done | bytes 262160
  735.7 24.2 %all_gather.15 = f32[128,512]{1,0:T(8,128)} all-gather(f32[8,512]{1,0:T(8,128)S(1)} %copy.45), channel_id=1, replica_groups=mesh['row'=16,'col'=16] {'col'}, dimensions={0}, use_global_device_ids=true | all-gather | bytes 278528 | tf_op jit(solution)/shard_map/all_gather | solution.py:15
  759.9 1.1 copy.46
  762.0 108.0 %all-reduce.17.cloned.1.call-done = f32[128,512]{0,1:T(8,128)} async-done(((f32[128,512]{0,1:T(8,128)}), f32[128,512]{0,1:T(8,128)}) %all-reduce.17.cloned.1.call-update) | async-done | bytes 262160 | tf_op jit(solution)/shard_map/psum | solution.py:11
  870.0 13.5 convolution_bitcast_fusion.1
  883.5 12.6 copy.47
  897.5 98.2 %reduce-scatter.7.cloned.1.call-done = f32[8,46,512]{2,1,0:T(8,128)} async-done(((f32[128,46,512]{2,1,0:T(8,128)}), f32[8,46,512]{2,1,0:T(8,128)}) %reduce-scatter.7.cloned.1.call-update) | async-done | bytes 753680 | tf_op jit(solution)/shard_map/reduce_scatter | solution.py:31
  995.7 1.3 slice_subtract_fusion
  997.2 3.0 convolution_bitcast_fusion.2
  1000.2 1.1 copy.50
  1001.4 255.4 %all-reduce.19.cloned.1.call-done = f32[512,512]{0,1:T(8,128)} async-done(((f32[512,512]{0,1:T(8,128)}), f32[512,512]{0,1:T(8,128)}) %all-reduce.19.cloned.1.call-update) | async-done | bytes 1048592 | tf_op jit(solution)/shard_map/psum | solution.py:58
  1256.8 2.5 broadcast_multiply_fusion
  1259.3 1.6 copy.49
  1262.1 11.7 cholesky.104
  1273.9 9.8 custom-call.31
  1283.8 1.2 constant_dynamic-update-slice_fusion.3
  1285.1 1.3 convolution_subtract_fusion.3
  1286.4 12.1 cholesky.217
  1298.6 9.8 custom-call.32
  1308.6 1.3 convolution_subtract_fusion.4
  1309.9 11.7 cholesky.238
  1322.4 9.8 custom-call.33
  1332.4 1.2 convolution_subtract_fusion.5
  1333.7 11.9 cholesky.255
  1349.6 10.5 while.1
  1350.3 2.0 bitcast_dynamic-update-slice_fusion.2
  1352.9 2.0 bitcast_dynamic-update-slice_fusion.2
  1355.5 2.0 bitcast_dynamic-update-slice_fusion.2
  1358.2 2.0 bitcast_dynamic-update-slice_fusion.2
  1360.1 40.2 %custom-call.34 = f32[4,128,128]{1,2,0:T(8,128)S(1)} custom-call(f32[4,128,128]{2,1,0:T(8,128)} %get-tuple-element.9), custom_call_target="InvertDiagBlocksLowerTriangular" | custom-call | tf_op jit(solution)/shard_map/jit(_solve_triangular)/triangular_solve | solution.py:61
  1401.4 1.6 convolution_subtract_fusion.1
  1403.4 1.6 convolution_subtract_fusion
  1406.3 2.3 copy.51
  (95 shorter events, 19.4 us)
Async XLA Ops:
  7.2 369.4 %copy-start = (f32[128,47,128]{2,0,1:T(8,128)S(1)}, f32[128,47,128]{2,0,1:T(8,128)}, u32[]{:S(2)}) copy-start(f32[128,47,128]{2,0,1:T(8,128)} %param.6) | copy-start | bytes 9240580
  7.2 135.5 %all-reduce.11.cloned.1.call-start = ((), (), s32[]{:S(2)}) async-start(), calls=%async_computation.2 | async-start | bytes 524288 | tf_op jit(solution)/shard_map/psum | solution.py:11
  33.0 208.1 %all-reduce.21.cloned.1.call-start = ((), (), s32[]{:S(2)}) async-start(), calls=%async_computation.9 | async-start | bytes 524288
  144.9 231.7 %all-reduce.13.cloned.1.call-start = ((), (), s32[]{:S(2)}) async-start(), calls=%async_computation.3 | async-start | bytes 524288 | tf_op jit(solution)/shard_map/psum | solution.py:11
  268.3 233.9 %reduce-scatter.5.cloned.1.call-start = ((), (), s32[]{:S(2)}) async-start(), calls=%async_computation.4 | async-start | bytes 13369344 | tf_op jit(solution)/shard_map/reduce_scatter | solution.py:31
  402.9 233.7 %copy-start.12 = (f32[2,128,128]{2,1,0:T(8,128)S(1)}, f32[2,128,128]{2,1,0:T(8,128)}, u32[]{:S(2)}) copy-start(f32[2,128,128]{2,1,0:T(8,128)} %param.8) | copy-start | bytes 393220
  402.9 467.1 %copy-start.3 = (f32[128,46,128]{2,0,1:T(8,128)S(1)}, f32[128,46,128]{2,0,1:T(8,128)}, u32[]{:S(2)}) copy-start(f32[128,46,128]{2,0,1:T(8,128)} %param.7) | copy-start | bytes 9043972
  402.9 233.6 %all-reduce.15.cloned.1.call-start = ((), (), s32[]{:S(2)}) async-start(), calls=%async_computation.5 | async-start | bytes 524288 | tf_op jit(solution)/shard_map/psum | solution.py:11
  503.8 0.9 copy-start.5
  527.9 206.7 %all-reduce.23.cloned.1.call-start = ((), (), s32[]{:S(2)}) async-start(), calls=%async_computation.10 | async-start | bytes 524288
  638.8 231.2 %all-reduce.17.cloned.1.call-start = ((), (), s32[]{:S(2)}) async-start(), calls=%async_computation.6 | async-start | bytes 524288 | tf_op jit(solution)/shard_map/psum | solution.py:11
  761.8 233.9 %reduce-scatter.7.cloned.1.call-start = ((), (), s32[]{:S(2)}) async-start(), calls=%async_computation.7 | async-start | bytes 13369344 | tf_op jit(solution)/shard_map/reduce_scatter | solution.py:31
  896.1 0.9 copy-start.10
  896.1 1.2 copy-start.11
  896.1 99.6 %copy-start.6 = (f32[8,47,512]{2,1,0:T(8,128)S(1)}, f32[8,47,512]{2,1,0:T(8,128)}, u32[]{:S(2)}) copy-start(f32[8,47,512]{2,1,0:T(8,128)} %copy-done.5) | copy-start | bytes 2310148
  896.1 101.0 %copy-start.13 = (f32[8,48]{1,0:T(8,128)S(1)}, f32[8,48]{1,0:T(8,128)}, u32[]{:S(2)}) copy-start(f32[8,48]{1,0:T(8,128)} %param.9) | copy-start | bytes 4612
  896.1 360.7 %all-reduce.19.cloned.1.call-start = ((), (), s32[]{:S(2)}) async-start(), calls=%async_computation.8 | async-start | bytes 2097152 | tf_op jit(solution)/shard_map/psum | solution.py:58
  997.2 262.1 %copy-start.2 = (f32[8,48,512]{2,1,0:T(8,128)}, f32[8,48,512]{2,1,0:T(8,128)S(1)}, u32[]{:S(2)}) copy-start(f32[8,48,512]{2,1,0:T(8,128)S(1)} %pad_maximum_fusion) | copy-start | bytes 2359300
  1256.8 4.0 copy-start.4
  1261.1 1.0 copy-start.9
  1285.0 115.3 %copy-start.7 = (f32[384,512]{0,1:T(8,128)S(1)}, f32[384,512]{0,1:T(8,128)}, u32[]{:S(2)}) copy-start(f32[384,512]{0,1:T(8,128)} %copy.50) | copy-start | bytes 2359300
  1360.1 40.6 %copy-start.8 = (f32[512,512]{1,0:T(8,128)}, f32[512,512]{1,0:T(8,128)S(1)}, u32[]{:S(2)}) copy-start(f32[512,512]{1,0:T(8,128)S(1)} %get-tuple-element.98) | copy-start | bytes 3145732
  1401.0 7.5 copy-start.1
Sparse Core Ops, SparseCore 0:
  33.2 109.4 all-reduce.10
  146.7 94.3 all-reduce.20
  268.5 108.0 all-reduce.12
  403.0 99.2 reduce-scatter.4
  528.0 108.5 all-reduce.14
  640.2 94.3 all-reduce.22
  761.9 108.0 all-reduce.16
  896.2 99.3 reduce-scatter.6
  1001.1 255.6 all-reduce.18
where the time goes:
time: 1420 us
  waiting for transfers between devices  1080 us (76%)
  other arithmetic  128 us (9%)
  blocking collectives  94.3 us (7%)
  local copies, waits for them, and re-layouts  52.5 us (4%)
  matrix products  45.1 us (3%)
  between operations  17.6 us (1%)
    psum x4, waiting for transfers between devices, spread(): return lax.psum(block, axis)  434 us
    psum x1, waiting for transfers between devices, body(): mass_gram = lax.psum(local_gram, ('row', 'col')) / ORDER  255 us
    reduce_scatter x2, waiting for transfers between devices, trailing(): lax.psum_scatter(jnp.einsum('jtq,qk->jtk', lower_tile, solved_cols, preci...  197 us
    unnamed x11, waiting for transfers between devices  190 us
    all_gather x4, blocking collectives, spread_rows(): grid_block = lax.all_gather(panel_rows, 'col', axis=0, tiled=True)  94.3 us
    another operation x14, other arithmetic, body(): factor = jnp.linalg.cholesky(mass_gram)  79 us
    another operation x3, other arithmetic, body(): jax.scipy.linalg.solve_triangular(factor, flattened.T, lower=True)  40.3 us
  transfers between devices with their start and end apart: 9, of which 9 were waited for; matrix products, arithmetic and copies ran while one was open for 0% of the time, Pallas kernels for 0%

commit v1 on v0

--- a/solution.py
+++ b/solution.py
@@ -55,7 +55,7 @@
     local_gram = jnp.einsum(
         "jtk,jtl->kl", weighted, solved, precision=highest, preferred_element_type=jnp.float32
     )
-    mass_gram = lax.psum(local_gram, ("row", "col")) / ORDER
+    mass_gram = lax.psum(lax.psum(local_gram, "row"), "col") / ORDER
     factor = jnp.linalg.cholesky(mass_gram)
     flattened = solved.reshape(-1, solved.shape[2])
     rotated = jax.scipy.linalg.solve_triangular(factor, flattened.T, lower=True).T

time: 1420 us -> 1380 us (0.972)
  waiting for transfers between devices: 1080 us -> 1030 us
    psum x1 -> x2, waiting for transfers between devices: 255 us -> 211 us  [body(): mass_gram = lax.psum(lax.psum(local_gram, 'row'), 'col') / ORDER]
    unnamed x11 -> x12, waiting for transfers between devices: 190 us -> 190 us
  transfers between devices with their start and end apart: 9 -> 10, of which waited for: 9 -> 10; matrix products, arithmetic and copies ran while one was open for 0% -> 0% of each run, Pallas kernels for 0% -> 0%
where the time goes in v1:
time: 1380 us; the launch traced here: 1370 us
  waiting for transfers between devices  1030 us (75%)
  other arithmetic  128 us (9%)
  blocking collectives  94.3 us (7%)
  local copies, waits for them, and re-layouts  51.6 us (4%)
  matrix products  44.9 us (3%)
  between operations  18 us (1%)
    psum x4, waiting for transfers between devices, spread(): return lax.psum(block, axis)  434 us
    psum x2, waiting for transfers between devices, body(): mass_gram = lax.psum(lax.psum(local_gram, 'row'), 'col') / ORDER  211 us
    reduce_scatter x2, waiting for transfers between devices, trailing(): lax.psum_scatter(jnp.einsum('jtq,qk->jtk', lower_tile, solved_cols, preci...  197 us
    unnamed x12, waiting for transfers between devices  190 us
    all_gather x4, blocking collectives, spread_rows(): grid_block = lax.all_gather(panel_rows, 'col', axis=0, tiled=True)  94.3 us
    another operation x14, other arithmetic, body(): factor = jnp.linalg.cholesky(mass_gram)  79 us
    another operation x3, other arithmetic, body(): jax.scipy.linalg.solve_triangular(factor, flattened.T, lower=True)  40.3 us
  transfers between devices with their start and end apart: 10, of which 10 were waited for; matrix products, arithmetic and copies ran while one was open for 0% of the time, Pallas kernels for 0%

profile of v1, /device:TPU:2, one launch (start us, length us, event | category | flops | bytes accessed | tf_op | source)
XLA Modules:
  0.0 1370.5 jit_solution(10562222523492336429)
XLA Ops:
  8.3 23.8 %all-gather = f32[128,1,512]{2,1,0:T(1,128)S(1)} all-gather(f32[8,1,512]{2,1,0:T(1,128)S(1)} %slice.132), channel_id=2, replica_groups=mesh['row'=16,'col'=16] {'col'}, dimensions={0}, use_global_device_ids=true | all-gather | bytes 278528 | tf_op jit(solution)/shard_map/all_gather | solution.py:15
  33.1 109.6 %all-reduce.12.cloned.1.call-done = f32[128,512]{1,0:T(8,128)} async-done(((f32[128,512]{1,0:T(8,128)}), f32[128,512]{1,0:T(8,128)}) %all-reduce.12.cloned.1.call-update) | async-done | bytes 262160 | tf_op jit(solution)/shard_map/psum | solution.py:11
  142.6 2.2 convolution_bitcast_fusion.4
  145.0 1.3 dynamic-slice.3
  146.9 94.3 %all-reduce.24.cloned.1.call-done = f32[128,512]{0,1:T(8,128)} async-done(((f32[128,512]{0,1:T(8,128)}), f32[128,512]{0,1:T(8,128)}) %all-reduce.24.cloned.1.call-update) | async-done | bytes 262160
  242.3 24.2 %all_gather.13 = f32[128,512]{1,0:T(8,128)} all-gather(f32[8,512]{1,0:T(8,128)S(1)} %copy.41), channel_id=1, replica_groups=mesh['row'=16,'col'=16] {'col'}, dimensions={0}, use_global_device_ids=true | all-gather | bytes 278528 | tf_op jit(solution)/shard_map/all_gather | solution.py:15
  266.5 1.1 copy.42
  268.4 108.2 %all-reduce.14.cloned.1.call-done = f32[128,512]{0,1:T(8,128)} async-done(((f32[128,512]{0,1:T(8,128)}), f32[128,512]{0,1:T(8,128)}) %all-reduce.14.cloned.1.call-update) | async-done | bytes 262160 | tf_op jit(solution)/shard_map/psum | solution.py:11
  376.6 13.6 convolution_bitcast_fusion
  390.2 12.7 copy.43
  403.0 99.3 %reduce-scatter.5.cloned.1.call-done = f32[8,47,512]{2,1,0:T(8,128)} async-done(((f32[128,47,512]{2,1,0:T(8,128)}), f32[8,47,512]{2,1,0:T(8,128)}) %reduce-scatter.5.cloned.1.call-update) | async-done | bytes 770064 | tf_op jit(solution)/shard_map/reduce_scatter | solution.py:31
  502.3 1.5 slice_subtract_fusion.1
  504.7 22.2 %all-gather.1 = f32[128,1,512]{2,1,0:T(1,128)S(1)} all-gather(f32[8,1,512]{2,1,0:T(1,128)S(1)} %slice.149), channel_id=3, replica_groups=mesh['row'=16,'col'=16] {'col'}, dimensions={0}, use_global_device_ids=true | all-gather | bytes 278528 | tf_op jit(solution)/shard_map/all_gather | solution.py:15
  527.9 108.6 %all-reduce.16.cloned.1.call-done = f32[128,512]{1,0:T(8,128)} async-done(((f32[128,512]{1,0:T(8,128)}), f32[128,512]{1,0:T(8,128)}) %all-reduce.16.cloned.1.call-update) | async-done | bytes 262160 | tf_op jit(solution)/shard_map/psum | solution.py:11
  636.6 2.2 convolution_bitcast_fusion.3
  638.9 95.7 %all-reduce.26.cloned.1.call-done = f32[128,512]{0,1:T(8,128)} async-done(((f32[128,512]{0,1:T(8,128)}), f32[128,512]{0,1:T(8,128)}) %all-reduce.26.cloned.1.call-update) | async-done | bytes 262160
  735.7 24.2 %all_gather.15 = f32[128,512]{1,0:T(8,128)} all-gather(f32[8,512]{1,0:T(8,128)S(1)} %copy.45), channel_id=1, replica_groups=mesh['row'=16,'col'=16] {'col'}, dimensions={0}, use_global_device_ids=true | all-gather | bytes 278528 | tf_op jit(solution)/shard_map/all_gather | solution.py:15
  759.9 1.1 copy.46
  762.0 108.0 %all-reduce.18.cloned.1.call-done = f32[128,512]{0,1:T(8,128)} async-done(((f32[128,512]{0,1:T(8,128)}), f32[128,512]{0,1:T(8,128)}) %all-reduce.18.cloned.1.call-update) | async-done | bytes 262160 | tf_op jit(solution)/shard_map/psum | solution.py:11
  870.0 13.5 convolution_bitcast_fusion.1
  883.5 12.6 copy.47
  897.5 98.2 %reduce-scatter.7.cloned.1.call-done = f32[8,46,512]{2,1,0:T(8,128)} async-done(((f32[128,46,512]{2,1,0:T(8,128)}), f32[8,46,512]{2,1,0:T(8,128)}) %reduce-scatter.7.cloned.1.call-update) | async-done | bytes 753680 | tf_op jit(solution)/shard_map/reduce_scatter | solution.py:31
  995.7 1.3 slice_subtract_fusion
  997.2 3.0 convolution_bitcast_fusion.2
  1000.4 111.0 %all-reduce.20.cloned.1.call-done = f32[512,512]{0,1:T(8,128)} async-done(((f32[512,512]{0,1:T(8,128)}), f32[512,512]{0,1:T(8,128)}) %all-reduce.20.cloned.1.call-update) | async-done | bytes 1048592 | tf_op jit(solution)/shard_map/psum | solution.py:58
  1111.8 100.0 %all-reduce.22.cloned.1.call-done = f32[512,512]{0,1:T(8,128)} async-done(((f32[512,512]{0,1:T(8,128)}), f32[512,512]{0,1:T(8,128)}) %all-reduce.22.cloned.1.call-update) | async-done | bytes 1048592 | tf_op jit(solution)/shard_map/psum | solution.py:58
  1211.9 2.5 broadcast_multiply_fusion
  1214.3 1.6 copy.49
  1217.1 11.7 cholesky.104
  1228.9 9.8 custom-call.31
  1238.8 1.2 constant_dynamic-update-slice_fusion.3
  1240.1 1.3 convolution_subtract_fusion.3
  1241.3 11.7 cholesky.217
  1253.1 10.2 custom-call.32
  1263.6 1.3 convolution_subtract_fusion.4
  1264.9 11.7 cholesky.238
  1277.3 9.8 custom-call.33
  1287.4 1.2 convolution_subtract_fusion.5
  1288.6 11.9 cholesky.255
  1304.5 10.5 while.1
  1305.2 2.0 bitcast_dynamic-update-slice_fusion.2
  1307.8 2.0 bitcast_dynamic-update-slice_fusion.2
  1310.4 2.0 bitcast_dynamic-update-slice_fusion.2
  1313.1 2.0 bitcast_dynamic-update-slice_fusion.2
  1315.0 40.2 %custom-call.34 = f32[4,128,128]{1,2,0:T(8,128)S(1)} custom-call(f32[4,128,128]{2,1,0:T(8,128)} %get-tuple-element.9), custom_call_target="InvertDiagBlocksLowerTriangular" | custom-call | tf_op jit(solution)/shard_map/jit(_solve_triangular)/triangular_solve | solution.py:61
  1356.3 1.6 convolution_subtract_fusion.1
  1358.3 1.6 convolution_subtract_fusion
  1361.2 2.3 copy.51
  (98 shorter events, 20.0 us)
Async XLA Ops:
  7.2 369.4 %copy-start = (f32[128,47,128]{2,0,1:T(8,128)S(1)}, f32[128,47,128]{2,0,1:T(8,128)}, u32[]{:S(2)}) copy-start(f32[128,47,128]{2,0,1:T(8,128)} %param.6) | copy-start | bytes 9240580
  7.2 135.5 %all-reduce.12.cloned.1.call-start = ((), (), s32[]{:S(2)}) async-start(), calls=%async_computation.2 | async-start | bytes 524288 | tf_op jit(solution)/shard_map/psum | solution.py:11
  33.0 208.1 %all-reduce.24.cloned.1.call-start = ((), (), s32[]{:S(2)}) async-start(), calls=%async_computation.10 | async-start | bytes 524288
  144.9 231.7 %all-reduce.14.cloned.1.call-start = ((), (), s32[]{:S(2)}) async-start(), calls=%async_computation.3 | async-start | bytes 524288 | tf_op jit(solution)/shard_map/psum | solution.py:11
  268.3 233.9 %reduce-scatter.5.cloned.1.call-start = ((), (), s32[]{:S(2)}) async-start(), calls=%async_computation.4 | async-start | bytes 13369344 | tf_op jit(solution)/shard_map/reduce_scatter | solution.py:31
  402.9 233.7 %copy-start.12 = (f32[2,128,128]{2,1,0:T(8,128)S(1)}, f32[2,128,128]{2,1,0:T(8,128)}, u32[]{:S(2)}) copy-start(f32[2,128,128]{2,1,0:T(8,128)} %param.8) | copy-start | bytes 393220
  402.9 467.1 %copy-start.3 = (f32[128,46,128]{2,0,1:T(8,128)S(1)}, f32[128,46,128]{2,0,1:T(8,128)}, u32[]{:S(2)}) copy-start(f32[128,46,128]{2,0,1:T(8,128)} %param.7) | copy-start | bytes 9043972
  402.9 233.6 %all-reduce.16.cloned.1.call-start = ((), (), s32[]{:S(2)}) async-start(), calls=%async_computation.5 | async-start | bytes 524288 | tf_op jit(solution)/shard_map/psum | solution.py:11
  503.8 0.9 copy-start.5
  527.9 206.7 %all-reduce.26.cloned.1.call-start = ((), (), s32[]{:S(2)}) async-start(), calls=%async_computation.11 | async-start | bytes 524288
  638.8 231.2 %all-reduce.18.cloned.1.call-start = ((), (), s32[]{:S(2)}) async-start(), calls=%async_computation.6 | async-start | bytes 524288 | tf_op jit(solution)/shard_map/psum | solution.py:11
  761.8 233.9 %reduce-scatter.7.cloned.1.call-start = ((), (), s32[]{:S(2)}) async-start(), calls=%async_computation.7 | async-start | bytes 13369344 | tf_op jit(solution)/shard_map/reduce_scatter | solution.py:31
  896.1 0.9 copy-start.10
  896.1 1.2 copy-start.11
  896.1 99.6 %copy-start.6 = (f32[8,47,512]{2,1,0:T(8,128)S(1)}, f32[8,47,512]{2,1,0:T(8,128)}, u32[]{:S(2)}) copy-start(f32[8,47,512]{2,1,0:T(8,128)} %copy-done.5) | copy-start | bytes 2310148
  896.1 101.0 %copy-start.13 = (f32[8,48]{1,0:T(8,128)S(1)}, f32[8,48]{1,0:T(8,128)}, u32[]{:S(2)}) copy-start(f32[8,48]{1,0:T(8,128)} %param.9) | copy-start | bytes 4612
  896.1 215.4 %all-reduce.20.cloned.1.call-start = ((), (), s32[]{:S(2)}) async-start(), calls=%async_computation.8 | async-start | bytes 2097152 | tf_op jit(solution)/shard_map/psum | solution.py:58
  997.2 114.7 %copy-start.2 = (f32[8,48,512]{2,1,0:T(8,128)}, f32[8,48,512]{2,1,0:T(8,128)S(1)}, u32[]{:S(2)}) copy-start(f32[8,48,512]{2,1,0:T(8,128)S(1)} %pad_maximum_fusion) | copy-start | bytes 2359300
  1000.2 211.7 %all-reduce.22.cloned.1.call-start = ((), (), s32[]{:S(2)}) async-start(), calls=%async_computation.9 | async-start | bytes 2097152 | tf_op jit(solution)/shard_map/psum | solution.py:58
  1111.8 243.8 %copy-start.7 = (f32[384,512]{0,1:T(8,128)}, f32[384,512]{0,1:T(8,128)S(1)}, u32[]{:S(2)}) copy-start(f32[384,512]{0,1:T(8,128)S(1)} %copy.50) | copy-start | bytes 2359300
  1211.9 4.0 copy-start.4
  1216.1 1.0 copy-start.9
  1315.0 40.6 %copy-start.8 = (f32[512,512]{1,0:T(8,128)}, f32[512,512]{1,0:T(8,128)S(1)}, u32[]{:S(2)}) copy-start(f32[512,512]{1,0:T(8,128)S(1)} %get-tuple-element.99) | copy-start | bytes 3145732
  1355.9 7.5 copy-start.1
Sparse Core Ops, SparseCore 0:
  33.2 109.4 all-reduce.11
  146.7 94.3 all-reduce.23
  268.5 108.0 all-reduce.13
  403.0 99.2 reduce-scatter.4
  528.0 108.5 all-reduce.15
  640.2 94.3 all-reduce.25
  761.9 108.0 all-reduce.17
  896.2 99.3 reduce-scatter.6
  1000.3 111.1 all-reduce.19
  1114.9 96.8 all-reduce.21
